TPU v7x, 128 devices: a whole 4x4x4 slice. The times are simulated.
128 devices in a mesh: str: 16 (over x_lo, y, core), crs: 8 (over x_hi, z).
Axes of the slice: x: 4 (x_hi: 2, x_lo: 2; x = x_hi * 2 + x_lo), y: 4, z: 4, core: 2. Of those that a mesh axis runs over, the one named last changes fastest.
Arguments:
- voltage: float32 [4, 512, 16384], P(None, 'str', 'crs'), may hold values from -4 to 0.5
- photocurrent: float32 [4, 512, 16384], P(None, 'str', 'crs'), may hold values from 0.1 to 10
- shunt: float32 [512, 16384], P('str', 'crs'), may hold values from 0.02 to 0.5
- series: float32 [512, 16384], P('str', 'crs'), may hold values from 0.5 to 2
- pattern: int32 [512, 128], P('str', 'crs'), may hold values from 0 to 3
- diode_mask: int32 [512, 128], P('str', 'crs'), may hold values 0 or 1
- aggregate: int32 [512, 128], P('str', 'crs'), may hold values from 0 to 4095, as said below
- coarse_inverse: float32 [4096, 4096], P('crs'), as said below
Outputs:
- newton_step: float32 [4, 512, 16384], P(None, 'str', 'crs')
- residual: float32 [4, 512, 16384], P(None, 'str', 'crs')
Inputs may be any that keep to these rules, and one draw needn't show every extreme that they name: `aggregate`: every value appears. coarse_inverse is symmetric positive definite.
All inputs are finite; a program needn't handle non-finite values. No bound on the sum of `diode_mask` on one device may be relied on, other than what follows from the above.
Results may differ from a plain program's by a relative error of at most 0.0003.
Values sent between devices are 32-bit elements; how exact they have to be, the bound alone decides.
A program may use at most 64 MiB of HBM per device.

v0:
```python
import jax
import jax.numpy as jnp
from jax import lax
from jax.sharding import PartitionSpec as P

ITERS = 3
LEVELS = (0.25, 0.5, 1.0, 2.0)
DIODE_SAT = 0.5


def with_halo(block, sides, width, periodic):
    for axis, dim in sides:
        count = lax.axis_size(axis)
        forward = [(i, i + 1) for i in range(count - 1)]
        if periodic:
            forward.append((count - 1, 0))
        backward = [(target, source) for source, target in forward]
        low = lax.ppermute(
            lax.slice_in_dim(block, block.shape[dim] - width, None, axis=dim), axis, forward
        )
        high = lax.ppermute(lax.slice_in_dim(block, 0, width, axis=dim), axis, backward)
        block = jnp.concatenate([low, block, high], axis=dim)
    return block


def widen(blocks):
    shape = blocks.shape
    spread = jnp.broadcast_to(blocks[..., None], shape + (128,))
    return spread.reshape(shape[:-1] + (shape[-1] * 128,))


def cross_levels(pattern):
    total = jnp.zeros(pattern.shape, jnp.float32)
    for number in range(4):
        total = total + jnp.where(pattern == number, jnp.float32(LEVELS[number]), jnp.float32(0.0))
    return total


def neighbours(field):
    along = with_halo(field, (("str", 1),), 1, True)
    across = with_halo(field, (("crs", 2),), 1, False)
    return (along[:, 2:], along[:, :-2], across[:, :, 2:], across[:, :, :-2])


def shards(voltage, photocurrent, shunt, series, pattern, diode_mask, aggregate, coarse_inverse):
    points = voltage.shape[0]
    rows_here = voltage.shape[1]
    local_block_list = voltage.shape[2] // 128
    coarse_count = coarse_inverse.shape[1]
    cross_level = widen(cross_levels(pattern))
    diode_area = widen(diode_mask.astype(jnp.float32))
    flat_groups = aggregate.reshape(-1)
    stacked = jnp.concatenate([voltage, cross_level[None], series[None]], axis=0)
    below, above, right_cells, left_cells = neighbours(stacked)
    right_link = jnp.minimum(cross_level, right_cells[points])
    left_link = jnp.minimum(cross_level, left_cells[points])
    up_link = above[points + 1]
    diode_derivative = DIODE_SAT * diode_area * jnp.exp(voltage)
    imbalance = (
        shunt * voltage
        + series * (voltage - below[:points])
        + up_link * (voltage - above[:points])
        + right_link * (voltage - right_cells[:points])
        + left_link * (voltage - left_cells[:points])
        + diode_derivative
        - DIODE_SAT * diode_area
        - photocurrent
    )
    diagonal = shunt + diode_derivative + series + up_link + right_link + left_link

    def restrict(remainder):
        block_sums = remainder.reshape(points, rows_here * local_block_list, 128).sum(axis=-1)
        return jax.ops.segment_sum(block_sums.T, flat_groups, num_segments=coarse_count).T

    def interpolate_upward(correction):
        picked = jnp.take(correction, flat_groups, axis=1)
        return widen(picked.reshape(points, rows_here, local_block_list))

    def coarse_solve(incomplete_value):
        product = None
        total = lax.psum(incomplete_value, ("str", "crs"))
        row_share = lax.dot_general(
            total, coarse_inverse, (((1,), (1,)), ((), ())), precision=lax.Precision.HIGHEST
        )
        correction = lax.all_gather(row_share, "crs", axis=1, tiled=True)
        return (correction, product)

    def precondition(remainder):
        resident_portion = remainder / diagonal
        incomplete_value = restrict(remainder)
        correction, product = coarse_solve(incomplete_value)
        smoothed = resident_portion + interpolate_upward(correction)
        product = lax.psum(jnp.sum(remainder * smoothed, axis=(1, 2)), ("str", "crs"))
        return (smoothed, product)

    remainder = -imbalance
    newton_step = jnp.zeros_like(voltage)
    smoothed, product = precondition(remainder)
    direction = smoothed
    for turn in range(ITERS):
        operate_below, operate_above, operate_right_cells, operate_left_cells = neighbours(
            direction
        )
        image = (
            diagonal * direction
            - series * operate_below
            - up_link * operate_above
            - right_link * operate_right_cells
            - left_link * operate_left_cells
        )
        curvature = lax.psum(jnp.sum(direction * image, axis=(1, 2)), ("str", "crs"))
        alpha = (product / curvature)[:, None, None]
        newton_step = newton_step + alpha * direction
        remainder = remainder - alpha * image
        if turn + 1 < ITERS:
            smoothed, fresh = precondition(remainder)
            ratio = (fresh / product)[:, None, None]
            direction = smoothed + ratio * direction
            product = fresh
    return (newton_step, remainder)


def solution(mesh):
    placed = (
        P(None, "str", "crs"),
        P(None, "str", "crs"),
        P("str", "crs"),
        P("str", "crs"),
        P("str", "crs"),
        P("str", "crs"),
        P("str", "crs"),
        P("crs", None),
    )
    return jax.shard_map(
        shards,
        mesh=mesh,
        in_specs=placed,
        out_specs=(P(None, "str", "crs"), P(None, "str", "crs")),
        check_vma=False,
    )
```

profile of v0, /device:TPU:1, one launch (start us, length us, event | category | flops | bytes accessed | tf_op | source)
XLA Modules:
  0.0 1062.8 jit_solution(3380685636923150555)
XLA Ops:
  8.3 1.2 pad_maximum_fusion.28
  9.5 1.5 collective-permute-start
  11.0 1.3 collective-permute-start.1
  12.4 1.3 collective-permute-start.2
  13.7 4.2 collective-permute-start.3
  20.6 2.9 fusion.30
  23.5 1.2 reshape.53
  24.8 1.6 reduce_sum.81
  26.5 3.8 scatter_custom_fusion
  30.4 158.7 %all-reduce.5.cloned.1.call-done = f32[4,4096]{0,1:T(8,128)} async-done(((f32[4,4096]{0,1:T(8,128)}), f32[4,4096]{0,1:T(8,128)}) %all-reduce.5.cloned.1.call-update) | async-done | bytes 65552 | tf_op jit(solution)/shard_map/psum | solution.py:81
  189.0 10.9 %fusion.54 = f32[4,512]{1,0:T(4,128)S(1)} fusion(f32[4,4096]{0,1:T(8,128)} %all-reduce.5.cloned.1.call-done, f32[512,4096]{1,0:T(8,128)} %param.17), kind=kOutput, calls=%fused_computation.118 | convolution fusion | flops 100663296 | bytes 8462336 | tf_op jit(solution)/shard_map/dot_general | solution.py:82
  199.9 28.1 %all_gather.9 = f32[4,4096]{1,0:T(4,128)S(1)} all-gather(f32[4,512]{1,0:T(4,128)S(1)} %fusion.54), channel_id=1, replica_groups=mesh['str'=16,'crs'=8] {'crs'}, dimensions={1}, use_global_device_ids=true | all-gather | bytes 73728 | tf_op jit(solution)/shard_map/all_gather | solution.py:85
  228.7 1.6 gather_fusion
  230.3 1.1 broadcast_select_fusion.2
  232.0 1.1 reshape.55
  233.2 2.6 divide_add_fusion.2
  235.8 7.2 collective-permute-start.4
  243.0 1.3 collective-permute-start.5
  244.3 1.3 collective-permute-start.6
  245.6 4.0 collective-permute-start.7
  249.7 1.8 collective-permute-done.7
  252.5 69.2 %all-reduce = (f32[4]{0:T(128)}, f32[4]{0:T(128)}) all-reduce(f32[4]{0:T(128)S(1)} %get-tuple-element.4, f32[4]{0:T(128)S(1)} %get-tuple-element.3), channel_id=1, replica_groups=mesh['str'=16,'crs'=8] {'str','crs'}, use_global_device_ids=true, to_apply=%region_4.6 | all-reduce | flops 8 | bytes 64 | tf_op jit(solution)/shard_map/psum | solution.py:93
  322.4 2.8 multiply_subtract_fusion.2
  325.2 1.4 reshape.56
  327.1 3.8 scatter_custom_fusion.1
  331.1 147.5 %all-reduce.7.cloned.1.call-done = f32[4,4096]{0,1:T(8,128)} async-done(((f32[4,4096]{0,1:T(8,128)}), f32[4,4096]{0,1:T(8,128)}) %all-reduce.7.cloned.1.call-update) | async-done | bytes 65552 | tf_op jit(solution)/shard_map/psum | solution.py:81
  478.6 10.9 %fusion.55 = f32[4,512]{1,0:T(4,128)S(1)} fusion(f32[4,4096]{0,1:T(8,128)} %all-reduce.7.cloned.1.call-done, f32[512,4096]{1,0:T(8,128)} %param.17), kind=kOutput, calls=%fused_computation.119 | convolution fusion | flops 100663296 | bytes 8462336 | tf_op jit(solution)/shard_map/dot_general | solution.py:82
  489.4 27.8 %all_gather.10 = f32[4,4096]{1,0:T(4,128)S(1)} all-gather(f32[4,512]{1,0:T(4,128)S(1)} %fusion.55), channel_id=1, replica_groups=mesh['str'=16,'crs'=8] {'crs'}, dimensions={1}, use_global_device_ids=true | all-gather | bytes 73728 | tf_op jit(solution)/shard_map/all_gather | solution.py:85
  517.2 2.0 copy.34
  519.2 3.3 gather_fusion.1
  522.6 1.8 broadcast_select_fusion.1
  524.3 1.2 copy.35
  525.6 1.3 broadcast_in_dim.100
  526.9 2.4 reshape.57
  529.3 1.6 multiply_reduce_fusion.3
  530.8 70.0 %psum.67 = f32[4]{0:T(128)S(1)} all-reduce(f32[4]{0:T(128)S(1)} %multiply_reduce_fusion.3), channel_id=1, replica_groups=mesh['str'=16,'crs'=8] {'str','crs'}, use_global_device_ids=true, to_apply=%region_11.13 | all-reduce | flops 4 | bytes 32 | tf_op jit(solution)/shard_map/psum | solution.py:93
  600.8 1.9 multiply_add_fusion.2
  602.8 1.2 collective-permute-start.8
  604.7 1.3 collective-permute-start.10
  606.0 4.0 collective-permute-start.11
  610.4 0.9 collective-permute-done.11
  613.3 71.4 %psum.68 = f32[4]{0:T(128)} all-reduce(f32[4]{0:T(128)S(1)} %multiply_reduce_fusion.2), channel_id=1, replica_groups=mesh['str'=16,'crs'=8] {'str','crs'}, use_global_device_ids=true, to_apply=%region_13.15 | all-reduce | flops 4 | bytes 32 | tf_op jit(solution)/shard_map/psum | solution.py:111
  685.4 3.1 multiply_subtract_fusion.1
  688.5 2.4 reshape.58
  690.8 1.6 reduce_sum.87
  693.3 4.1 scatter_custom_fusion.2
  697.3 147.4 %all-reduce.9.cloned.1.call-done = f32[4,4096]{0,1:T(8,128)} async-done(((f32[4,4096]{0,1:T(8,128)}), f32[4,4096]{0,1:T(8,128)}) %all-reduce.9.cloned.1.call-update) | async-done | bytes 65552 | tf_op jit(solution)/shard_map/psum | solution.py:81
  844.8 10.9 %fusion.56 = f32[4,512]{1,0:T(4,128)S(1)} fusion(f32[4,4096]{0,1:T(8,128)} %all-reduce.9.cloned.1.call-done, f32[512,4096]{1,0:T(8,128)} %param.17), kind=kOutput, calls=%fused_computation.120 | convolution fusion | flops 100663296 | bytes 8462336 | tf_op jit(solution)/shard_map/dot_general | solution.py:82
  855.6 27.8 %all_gather.11 = f32[4,4096]{1,0:T(4,128)S(1)} all-gather(f32[4,512]{1,0:T(4,128)S(1)} %fusion.56), channel_id=1, replica_groups=mesh['str'=16,'crs'=8] {'crs'}, dimensions={1}, use_global_device_ids=true | all-gather | bytes 73728 | tf_op jit(solution)/shard_map/all_gather | solution.py:85
  883.4 2.0 copy.37
  885.4 3.2 gather_fusion.2
  888.6 1.8 broadcast_select_fusion
  890.4 1.2 copy.38
  891.7 1.3 broadcast_in_dim.102
  893.0 2.4 reshape.59
  895.4 1.9 multiply_reduce_fusion.1
  897.2 70.1 %psum.70 = f32[4]{0:T(128)S(1)} all-reduce(f32[4]{0:T(128)S(1)} %multiply_reduce_fusion.1), channel_id=1, replica_groups=mesh['str'=16,'crs'=8] {'str','crs'}, use_global_device_ids=true, to_apply=%region_18.20 | all-reduce | flops 4 | bytes 32 | tf_op jit(solution)/shard_map/psum | solution.py:93
  967.4 1.9 multiply_add_fusion.1
  969.4 1.2 collective-permute-start.12
  971.3 1.3 collective-permute-start.14
  972.6 4.0 collective-permute-start.15
  979.9 71.0 %psum.71 = f32[4]{0:T(128)} all-reduce(f32[4]{0:T(128)S(1)} %multiply_reduce_fusion), channel_id=1, replica_groups=mesh['str'=16,'crs'=8] {'str','crs'}, use_global_device_ids=true, to_apply=%region_20.22 | all-reduce | flops 4 | bytes 32 | tf_op jit(solution)/shard_map/psum | solution.py:111
  1051.6 2.7 multiply_add_fusion
  1054.3 1.7 multiply_subtract_fusion
  (144 shorter events, 17.3 us)
Async XLA Ops:
  7.2 5.2 copy-start.1
  7.2 5.1 copy-start
  7.2 181.9 %all-reduce.5.cloned.1.call-start = ((), (), s32[]{:S(2)}) async-start(), calls=%async_computation | async-start | bytes 4194304 | tf_op jit(solution)/shard_map/psum | solution.py:81
  8.1 9.8 copy-start.39
  8.1 9.8 copy-start.37
  9.5 10.3 collective-permute-start
  11.0 8.6 collective-permute-start.1
  12.4 7.1 collective-permute-start.2
  13.7 5.8 collective-permute-start.3
  18.1 0.6 copy-start.35
  19.5 1.1 copy-start.24
  19.5 0.7 copy-start.25
  19.8 3.7 copy-start.7
  19.8 3.7 copy-start.12
  19.8 3.7 copy-start.17
  19.8 0.7 copy-start.34
  23.5 6.8 copy-start.3
  26.5 3.9 copy-start.38
  30.3 448.3 %all-reduce.7.cloned.1.call-start = ((), (), s32[]{:S(2)}) async-start(), calls=%async_computation.1 | async-start | bytes 4194304 | tf_op jit(solution)/shard_map/psum | solution.py:81
  199.9 30.4 %copy-start.36 = (pred[512]{0:T(512)(128)(4,1)S(1)}, pred[512]{0:T(512)(128)(4,1)}, u32[]{:S(2)}) copy-start(pred[512]{0:T(512)(128)(4,1)} %compare_and_fusion) | copy-start | bytes 1540
  233.2 18.4 %copy-start.4 = (f32[4,32,2048]{2,1,0:T(8,128)S(1)}, f32[4,32,2048]{2,1,0:T(8,128)}, u32[]{:S(2)}) copy-start(f32[4,32,2048]{2,1,0:T(8,128)} %copy-done.3) | copy-start | bytes 3145732
  233.2 18.4 %copy-start.8 = (f32[32,2048]{1,0:T(8,128)S(1)}, f32[32,2048]{1,0:T(8,128)}, u32[]{:S(2)}) copy-start(f32[32,2048]{1,0:T(8,128)} %copy-done.7) | copy-start | bytes 786436
  233.2 18.4 %copy-start.13 = (f32[32,2048]{1,0:T(8,128)S(1)}, f32[32,2048]{1,0:T(8,128)}, u32[]{:S(2)}) copy-start(f32[32,2048]{1,0:T(8,128)} %copy-done.12) | copy-start | bytes 786436
  233.2 18.4 %copy-start.18 = (f32[32,2048]{1,0:T(8,128)S(1)}, f32[32,2048]{1,0:T(8,128)}, u32[]{:S(2)}) copy-start(f32[32,2048]{1,0:T(8,128)} %copy-done.17) | copy-start | bytes 786436
  235.8 15.7 %collective-permute-start.4 = (f32[4,1,2048]{2,1,0:T(1,128)S(1)}, f32[4,1,2048]{2,1,0:T(1,128)S(1)}, u32[]{:S(2)}, u32[]{:S(2)}) collective-permute-start(f32[4,1,2048]{2,1,0:T(1,128)S(1)} %get-tuple-element.24), channel_id=1, source_target_pairs={{8,0},{16,8},{24,16},{32,24},{40,32},{48,40},{56,48},{64,56},{72,6... | collective-permute-start | bytes 98312 | tf_op jit(solution)/shard_map/ppermute | solution.py:21
  243.0 8.6 collective-permute-start.5
  244.3 5.4 collective-permute-start.6
  245.6 5.9 collective-permute-start.7
  251.5 1.0 copy-start.28
  251.5 1.0 copy-start.31
  251.6 70.8 %copy-start.5 = (f32[4,32,2048]{2,1,0:T(8,128)S(1)}, f32[4,32,2048]{2,1,0:T(8,128)}, u32[]{:S(2)}) copy-start(f32[4,32,2048]{2,1,0:T(8,128)} %copy-done.3) | copy-start | bytes 3145732
  330.9 513.9 %all-reduce.9.cloned.1.call-start = ((), (), s32[]{:S(2)}) async-start(), calls=%async_computation.2 | async-start | bytes 4194304 | tf_op jit(solution)/shard_map/psum | solution.py:81
  519.2 10.0 copy-start.6
  529.3 71.5 %copy-start.42 = (f32[4]{0:T(128)S(1)}, f32[4]{0:T(128)}, u32[]{:S(2)}) copy-start(f32[4]{0:T(128)} %get-tuple-element.5) | copy-start | bytes 52
  600.8 2.0 copy-start.40
  600.8 11.7 %copy-start.9 = (f32[32,2048]{1,0:T(8,128)S(1)}, f32[32,2048]{1,0:T(8,128)}, u32[]{:S(2)}) copy-start(f32[32,2048]{1,0:T(8,128)} %copy-done.7) | copy-start | bytes 786436
  600.8 11.7 %copy-start.14 = (f32[32,2048]{1,0:T(8,128)S(1)}, f32[32,2048]{1,0:T(8,128)}, u32[]{:S(2)}) copy-start(f32[32,2048]{1,0:T(8,128)} %copy-done.12) | copy-start | bytes 786436
  600.8 11.7 %copy-start.19 = (f32[32,2048]{1,0:T(8,128)S(1)}, f32[32,2048]{1,0:T(8,128)}, u32[]{:S(2)}) copy-start(f32[32,2048]{1,0:T(8,128)} %copy-done.17) | copy-start | bytes 786436
  602.8 8.5 collective-permute-start.8
  604.0 7.3 collective-permute-start.9
  604.7 5.7 collective-permute-start.10
  606.0 5.3 collective-permute-start.11
  611.3 0.6 copy-start.32
  611.9 0.6 copy-start.33
  895.4 72.0 %copy-start.41 = (f32[4]{0:T(128)S(1)}, f32[4]{0:T(128)}, u32[]{:S(2)}) copy-start(f32[4]{0:T(128)} %copy-done.40) | copy-start | bytes 52
  967.4 11.7 %copy-start.10 = (f32[32,2048]{1,0:T(8,128)S(1)}, f32[32,2048]{1,0:T(8,128)}, u32[]{:S(2)}) copy-start(f32[32,2048]{1,0:T(8,128)} %copy-done.7) | copy-start | bytes 786436
  967.4 11.7 %copy-start.15 = (f32[32,2048]{1,0:T(8,128)S(1)}, f32[32,2048]{1,0:T(8,128)}, u32[]{:S(2)}) copy-start(f32[32,2048]{1,0:T(8,128)} %copy-done.12) | copy-start | bytes 786436
  967.4 11.7 %copy-start.20 = (f32[32,2048]{1,0:T(8,128)S(1)}, f32[32,2048]{1,0:T(8,128)}, u32[]{:S(2)}) copy-start(f32[32,2048]{1,0:T(8,128)} %copy-done.17) | copy-start | bytes 786436
  969.3 8.6 copy-start.22
  969.4 8.5 collective-permute-start.12
  970.5 7.3 collective-permute-start.13
  971.3 5.7 collective-permute-start.14
  972.6 5.3 collective-permute-start.15
  977.9 0.6 copy-start.26
  978.5 0.6 copy-start.29
  1051.6 2.7 copy-start.2
  1051.6 2.7 copy-start.11
  1051.6 2.7 copy-start.16
  1051.6 2.7 copy-start.21
  1051.6 2.7 copy-start.23
  1051.6 2.7 copy-start.27
  1051.6 2.7 copy-start.30
Sparse Core Ops, SparseCore 0:
  30.4 158.5 all-reduce.4
  331.0 147.5 all-reduce.6
  697.5 147.2 all-reduce.8
where the time goes:
time: 1070 us; the launch traced here: 1060 us
  waiting for transfers between devices  458 us (43%)
  blocking collectives  435 us (41%)
  other arithmetic  50.6 us (5%)
  starting transfers between devices  36.5 us (3%)
  local copies, waits for them, and re-layouts  35 us (3%)
  matrix products  32.6 us (3%)
  between operations  14.5 us (1%)
    psum x3, waiting for transfers between devices, coarse_solve(): total = lax.psum(incomplete_value, ('str', 'crs'))  454 us
    psum x3, blocking collectives, precondition(): lax.psum(jnp.sum(remainder * smoothed, axis=(1, 2)), ('str', 'crs'))  209 us
    psum x2, blocking collectives, shards(): lax.psum(jnp.sum(direction * image, axis=(1, 2)), ('str', 'crs'))  142 us
    all_gather x3, blocking collectives, coarse_solve(): correction = lax.all_gather(row_share, 'crs', axis=1, tiled=True)  83.8 us
    dot_general x3, matrix products, coarse_solve(): lax.dot_general(total, coarse_inverse, (((1,), (1,)), ((), ())), precisio...  32.6 us
  transfers between devices with their start and end apart: 19, of which 9 were waited for; matrix products, arithmetic and copies ran while one was open for 0% of the time, Pallas kernels for 0%

commit v1 on v0

--- a/solution.py
+++ b/solution.py
@@ -82,7 +82,9 @@
         row_share = lax.dot_general(
             total, coarse_inverse, (((1,), (1,)), ((), ())), precision=lax.Precision.HIGHEST
         )
-        correction = lax.all_gather(row_share, "crs", axis=1, tiled=True)
+        correction = jnp.concatenate(
+            lax.all_to_all(jnp.stack([row_share] * lax.axis_size("crs")), "crs", 0, 0), axis=1
+        )
         return (correction, product)
 
     def precondition(remainder):

time: 1070 us -> 1010 us (0.944)
  blocking collectives: 435 us -> 365 us
    all_gather x3 -> x0, blocking collectives: 83.8 us -> none  [coarse_solve(): correction = lax.all_gather(row_share, 'crs', axis=1, tiled=True)]
    all_to_all x0 -> x2, blocking collectives: none -> 23.6 us  [coarse_solve(): lax.all_to_all(jnp.stack([row_share] * lax.axis_size('crs')), 'crs', 0, 0)]
  transfers between devices with their start and end apart: 19 -> 20, of which waited for: 9 -> 10; matrix products, arithmetic and copies ran while one was open for 0% -> 0% of each run, Pallas kernels for 0% -> 0%
where the time goes in v1:
time: 1010 us; the launch traced here: 998 us
  waiting for transfers between devices  464 us (46%)
  blocking collectives  365 us (36%)
  other arithmetic  50.9 us (5%)
  local copies, waits for them, and re-layouts  36.8 us (4%)
  starting transfers between devices  35.4 us (4%)
  matrix products  32.6 us (3%)
  between operations  14.6 us (1%)
    psum x3, waiting for transfers between devices, coarse_solve(): total = lax.psum(incomplete_value, ('str', 'crs'))  453 us
    psum x3, blocking collectives, precondition(): lax.psum(jnp.sum(remainder * smoothed, axis=(1, 2)), ('str', 'crs'))  199 us
    psum x2, blocking collectives, shards(): lax.psum(jnp.sum(direction * image, axis=(1, 2)), ('str', 'crs'))  142 us
    dot_general x3, matrix products, coarse_solve(): lax.dot_general(total, coarse_inverse, (((1,), (1,)), ((), ())), precisio...  32.6 us
    all_to_all x2, blocking collectives, coarse_solve(): lax.all_to_all(jnp.stack([row_share] * lax.axis_size('crs')), 'crs', 0, 0)  23.6 us
  transfers between devices with their start and end apart: 20, of which 10 were waited for; matrix products, arithmetic and copies ran while one was open for 0% of the time, Pallas kernels for 0%

profile of v1, /device:TPU:1, one launch (start us, length us, event | category | flops | bytes accessed | tf_op | source)
XLA Modules:
  0.0 998.4 jit_solution(7587649811188228826)
XLA Ops:
  8.3 1.2 pad_maximum_fusion.28
  9.5 1.5 collective-permute-start
  11.0 1.3 collective-permute-start.1
  12.4 1.3 collective-permute-start.2
  13.7 4.2 collective-permute-start.3
  20.6 2.9 fusion.30
  23.5 1.2 reshape.77
  24.8 1.6 reduce_sum.81
  26.5 3.6 scatter_custom_fusion
  30.2 158.7 %all-reduce.5.cloned.1.call-done = f32[4,4096]{0,1:T(8,128)} async-done(((f32[4,4096]{0,1:T(8,128)}), f32[4,4096]{0,1:T(8,128)}) %all-reduce.5.cloned.1.call-update) | async-done | bytes 65552 | tf_op jit(solution)/shard_map/psum | solution.py:81
  188.9 10.9 %fusion.54 = f32[4,512]{1,0:T(4,128)S(1)} fusion(f32[4,4096]{0,1:T(8,128)} %all-reduce.5.cloned.1.call-done, f32[512,4096]{1,0:T(8,128)} %param.17), kind=kOutput, calls=%fused_computation.118 | convolution fusion | flops 100663296 | bytes 8462336 | tf_op jit(solution)/shard_map/dot_general | solution.py:82
  200.4 5.3 all-to-all-start
  206.0 6.5 all-to-all-done
  213.1 1.6 gather_fusion
  214.7 1.1 broadcast_select_fusion.2
  216.4 1.1 reshape.81
  217.6 2.6 divide_add_fusion.2
  220.2 1.5 collective-permute-start.4
  222.1 1.3 collective-permute-start.6
  223.4 4.0 collective-permute-start.7
  227.5 1.2 collective-permute-done.7
  228.8 1.4 multiply_reduce_fusion.4
  230.2 71.2 %all-reduce = (f32[4]{0:T(128)}, f32[4]{0:T(128)}) all-reduce(f32[4]{0:T(128)} %get-tuple-element.4, f32[4]{0:T(128)S(1)} %get-tuple-element.3), channel_id=1, replica_groups=mesh['str'=16,'crs'=8] {'str','crs'}, use_global_device_ids=true, to_apply=%region_4.6 | all-reduce | flops 8 | bytes 64 | tf_op jit(solution)/shard_map/psum | solution.py:95
  302.1 2.8 multiply_subtract_fusion.2
  304.9 1.4 reshape.82
  306.8 3.6 scatter_custom_fusion.1
  310.7 147.2 %all-reduce.7.cloned.1.call-done = f32[4,4096]{0,1:T(8,128)} async-done(((f32[4,4096]{0,1:T(8,128)}), f32[4,4096]{0,1:T(8,128)}) %all-reduce.7.cloned.1.call-update) | async-done | bytes 65552 | tf_op jit(solution)/shard_map/psum | solution.py:81
  457.9 10.9 %fusion.55 = f32[4,512]{1,0:T(4,128)S(1)} fusion(f32[4,4096]{0,1:T(8,128)} %all-reduce.7.cloned.1.call-done, f32[512,4096]{1,0:T(8,128)} %param.17), kind=kOutput, calls=%fused_computation.119 | convolution fusion | flops 100663296 | bytes 8462336 | tf_op jit(solution)/shard_map/dot_general | solution.py:82
  468.8 11.8 %all_to_all.15 = f32[8,4,512]{2,1,0:T(4,128)S(1)} all-to-all(f32[8,4,512]{2,1,0:T(4,128)S(1)} %stack.7), channel_id=1, replica_groups=mesh['str'=16,'crs'=8] {'crs'}, dimensions={0} | all-to-all | bytes 131072 | tf_op jit(solution)/shard_map/all_to_all | solution.py:86
  480.6 2.0 copy.34
  482.6 3.3 gather_fusion.1
  485.9 1.8 broadcast_select_fusion.1
  487.7 1.2 copy.35
  489.0 1.3 broadcast_in_dim.100
  490.3 2.4 reshape.85
  492.7 1.6 multiply_reduce_fusion.3
  494.2 63.6 %psum.67 = f32[4]{0:T(128)S(1)} all-reduce(f32[4]{0:T(128)S(1)} %multiply_reduce_fusion.3), channel_id=1, replica_groups=mesh['str'=16,'crs'=8] {'str','crs'}, use_global_device_ids=true, to_apply=%region_11.13 | all-reduce | flops 4 | bytes 32 | tf_op jit(solution)/shard_map/psum | solution.py:95
  557.9 1.9 multiply_add_fusion.2
  559.9 1.0 collective-permute-start.8
  561.8 1.3 collective-permute-start.10
  563.1 4.0 collective-permute-start.11
  569.6 1.3 multiply_reduce_fusion.2
  571.0 71.4 %psum.68 = f32[4]{0:T(128)} all-reduce(f32[4]{0:T(128)} %multiply_reduce_fusion.2), channel_id=1, replica_groups=mesh['str'=16,'crs'=8] {'str','crs'}, use_global_device_ids=true, to_apply=%region_13.15 | all-reduce | flops 4 | bytes 32 | tf_op jit(solution)/shard_map/psum | solution.py:113
  643.6 3.1 multiply_subtract_fusion.1
  646.7 2.4 reshape.86
  649.0 1.6 reduce_sum.87
  651.5 4.0 scatter_custom_fusion.2
  655.5 147.2 %all-reduce.9.cloned.1.call-done = f32[4,4096]{0,1:T(8,128)} async-done(((f32[4,4096]{0,1:T(8,128)}), f32[4,4096]{0,1:T(8,128)}) %all-reduce.9.cloned.1.call-update) | async-done | bytes 65552 | tf_op jit(solution)/shard_map/psum | solution.py:81
  802.7 10.9 %fusion.56 = f32[4,512]{1,0:T(4,128)S(1)} fusion(f32[4,4096]{0,1:T(8,128)} %all-reduce.9.cloned.1.call-done, f32[512,4096]{1,0:T(8,128)} %param.17), kind=kOutput, calls=%fused_computation.120 | convolution fusion | flops 100663296 | bytes 8462336 | tf_op jit(solution)/shard_map/dot_general | solution.py:82
  813.6 11.8 %all_to_all.16 = f32[8,4,512]{2,1,0:T(4,128)S(1)} all-to-all(f32[8,4,512]{2,1,0:T(4,128)S(1)} %stack.8), channel_id=1, replica_groups=mesh['str'=16,'crs'=8] {'crs'}, dimensions={0} | all-to-all | bytes 131072 | tf_op jit(solution)/shard_map/all_to_all | solution.py:86
  825.4 2.0 copy.37
  827.4 3.2 gather_fusion.2
  830.6 1.8 broadcast_select_fusion
  832.4 1.2 copy.38
  833.6 1.3 broadcast_in_dim.102
  834.9 2.4 reshape.89
  837.3 1.9 multiply_reduce_fusion.1
  839.2 63.8 %psum.70 = f32[4]{0:T(128)S(1)} all-reduce(f32[4]{0:T(128)S(1)} %multiply_reduce_fusion.1), channel_id=1, replica_groups=mesh['str'=16,'crs'=8] {'str','crs'}, use_global_device_ids=true, to_apply=%region_18.20 | all-reduce | flops 4 | bytes 32 | tf_op jit(solution)/shard_map/psum | solution.py:95
  903.0 1.9 multiply_add_fusion.1
  906.9 1.3 collective-permute-start.14
  908.2 4.0 collective-permute-start.15
  915.6 70.9 %psum.71 = f32[4]{0:T(128)} all-reduce(f32[4]{0:T(128)S(1)} %multiply_reduce_fusion), channel_id=1, replica_groups=mesh['str'=16,'crs'=8] {'str','crs'}, use_global_device_ids=true, to_apply=%region_20.22 | all-reduce | flops 4 | bytes 32 | tf_op jit(solution)/shard_map/psum | solution.py:113
  987.2 2.7 multiply_add_fusion
  990.0 1.7 multiply_subtract_fusion
  (152 shorter events, 19.8 us)
Async XLA Ops:
  7.2 5.2 copy-start.1
  7.2 5.1 copy-start
  7.2 181.7 %all-reduce.5.cloned.1.call-start = ((), (), s32[]{:S(2)}) async-start(), calls=%async_computation.3 | async-start | bytes 4194304 | tf_op jit(solution)/shard_map/psum | solution.py:81
  8.1 9.8 copy-start.39
  8.1 9.8 copy-start.37
  9.5 10.4 %collective-permute-start = (f32[6,1,2048]{2,1,0:T(1,128)S(1)}, f32[6,1,2048]{2,1,0:T(1,128)S(1)}, u32[]{:S(2)}, u32[]{:S(2)}) collective-permute-start(f32[6,1,2048]{2,1,0:T(1,128)S(1)} %get-tuple-element.12), channel_id=1, source_target_pairs={{8,0},{16,8},{24,16},{32,24},{40,32},{48,40},{56,48},{64,56},{72,6... | collective-permute-start | bytes 147464 | tf_op jit(solution)/shard_map/ppermute | solution.py:21
  11.0 8.6 collective-permute-start.1
  12.4 7.1 collective-permute-start.2
  13.7 5.9 collective-permute-start.3
  18.1 0.6 copy-start.35
  19.5 1.0 copy-start.24
  19.6 0.7 copy-start.25
  19.8 3.7 copy-start.7
  19.8 3.7 copy-start.12
  19.8 3.7 copy-start.17
  19.9 0.7 copy-start.34
  23.5 6.7 copy-start.2
  23.5 3.0 copy-start.36
  30.2 175.7 %copy-start.38 = (s32[512]{0:T(512)S(1)}, s32[512]{0:T(512)}, u32[]{:S(2)}) copy-start(s32[512]{0:T(512)} %compare_select_fusion) | copy-start | bytes 6148
  200.4 12.0 %all-to-all-start = ((f32[8,4,512]{2,1,0:T(4,128)}), f32[8,4,512]{2,1,0:T(4,128)S(1)}, u32[]{:S(2)}, u32[]{:S(2)}) async-start(f32[8,4,512]{2,1,0:T(4,128)} %stack.6), calls=%async_computation | async-start | bytes 131072 | tf_op jit(solution)/shard_map/all_to_all | solution.py:86
  205.7 252.2 %all-reduce.7.cloned.1.call-start = ((), (), s32[]{:S(2)}) async-start(), calls=%async_computation.4 | async-start | bytes 4194304 | tf_op jit(solution)/shard_map/psum | solution.py:81
  217.6 11.1 %copy-start.3 = (f32[4,32,2048]{2,1,0:T(8,128)S(1)}, f32[4,32,2048]{2,1,0:T(8,128)}, u32[]{:S(2)}) copy-start(f32[4,32,2048]{2,1,0:T(8,128)} %copy-done.2) | copy-start | bytes 3145732
  217.6 11.2 %copy-start.8 = (f32[32,2048]{1,0:T(8,128)S(1)}, f32[32,2048]{1,0:T(8,128)}, u32[]{:S(2)}) copy-start(f32[32,2048]{1,0:T(8,128)} %copy-done.7) | copy-start | bytes 786436
  217.6 11.2 %copy-start.13 = (f32[32,2048]{1,0:T(8,128)S(1)}, f32[32,2048]{1,0:T(8,128)}, u32[]{:S(2)}) copy-start(f32[32,2048]{1,0:T(8,128)} %copy-done.12) | copy-start | bytes 786436
  217.6 11.2 %copy-start.18 = (f32[32,2048]{1,0:T(8,128)S(1)}, f32[32,2048]{1,0:T(8,128)}, u32[]{:S(2)}) copy-start(f32[32,2048]{1,0:T(8,128)} %copy-done.17) | copy-start | bytes 786436
  220.2 8.5 collective-permute-start.4
  221.7 7.0 collective-permute-start.5
  222.1 5.4 collective-permute-start.6
  223.4 5.3 collective-permute-start.7
  228.7 1.5 copy-start.28
  228.7 1.5 copy-start.31
  228.8 73.3 %copy-start.4 = (f32[4,32,2048]{2,1,0:T(8,128)S(1)}, f32[4,32,2048]{2,1,0:T(8,128)}, u32[]{:S(2)}) copy-start(f32[4,32,2048]{2,1,0:T(8,128)} %copy-done.2) | copy-start | bytes 3145732
  310.4 492.2 %all-reduce.9.cloned.1.call-start = ((), (), s32[]{:S(2)}) async-start(), calls=%async_computation.5 | async-start | bytes 4194304 | tf_op jit(solution)/shard_map/psum | solution.py:81
  482.6 10.0 %copy-start.6 = (f32[4,32,2048]{2,1,0:T(8,128)S(1)}, f32[4,32,2048]{2,1,0:T(8,128)}, u32[]{:S(2)}) copy-start(f32[4,32,2048]{2,1,0:T(8,128)} %multiply_subtract_fusion.2) | copy-start | bytes 3145732
  492.7 65.2 %copy-start.44 = (f32[4]{0:T(128)S(1)}, f32[4]{0:T(128)}, u32[]{:S(2)}) copy-start(f32[4]{0:T(128)} %get-tuple-element.5) | copy-start | bytes 52
  557.9 2.0 copy-start.42
  557.9 11.8 %copy-start.9 = (f32[32,2048]{1,0:T(8,128)S(1)}, f32[32,2048]{1,0:T(8,128)}, u32[]{:S(2)}) copy-start(f32[32,2048]{1,0:T(8,128)} %copy-done.7) | copy-start | bytes 786436
  557.9 11.8 %copy-start.14 = (f32[32,2048]{1,0:T(8,128)S(1)}, f32[32,2048]{1,0:T(8,128)}, u32[]{:S(2)}) copy-start(f32[32,2048]{1,0:T(8,128)} %copy-done.12) | copy-start | bytes 786436
  557.9 11.8 %copy-start.19 = (f32[32,2048]{1,0:T(8,128)S(1)}, f32[32,2048]{1,0:T(8,128)}, u32[]{:S(2)}) copy-start(f32[32,2048]{1,0:T(8,128)} %copy-done.17) | copy-start | bytes 786436
  559.9 8.5 collective-permute-start.8
  560.9 7.5 collective-permute-start.9
  561.8 5.7 collective-permute-start.10
  563.1 5.3 collective-permute-start.11
  568.4 0.6 copy-start.32
  569.0 0.6 copy-start.33
  837.3 65.7 %copy-start.43 = (f32[4]{0:T(128)S(1)}, f32[4]{0:T(128)}, u32[]{:S(2)}) copy-start(f32[4]{0:T(128)} %copy-done.42) | copy-start | bytes 52
  903.0 11.8 %copy-start.10 = (f32[32,2048]{1,0:T(8,128)S(1)}, f32[32,2048]{1,0:T(8,128)}, u32[]{:S(2)}) copy-start(f32[32,2048]{1,0:T(8,128)} %copy-done.7) | copy-start | bytes 786436
  903.0 11.8 %copy-start.15 = (f32[32,2048]{1,0:T(8,128)S(1)}, f32[32,2048]{1,0:T(8,128)}, u32[]{:S(2)}) copy-start(f32[32,2048]{1,0:T(8,128)} %copy-done.12) | copy-start | bytes 786436
  903.0 11.8 %copy-start.20 = (f32[32,2048]{1,0:T(8,128)S(1)}, f32[32,2048]{1,0:T(8,128)}, u32[]{:S(2)}) copy-start(f32[32,2048]{1,0:T(8,128)} %copy-done.17) | copy-start | bytes 786436
  905.0 8.6 copy-start.22
  905.0 82.2 %copy-start.41 = (f32[4]{0:T(128)S(1)}, f32[4]{0:T(128)}, u32[]{:S(2)}) copy-start(f32[4]{0:T(128)} %copy-done.40) | copy-start | bytes 52
  905.0 8.5 collective-permute-start.12
  906.0 7.5 collective-permute-start.13
  906.9 5.7 collective-permute-start.14
  908.2 5.3 collective-permute-start.15
  913.6 0.6 copy-start.26
  914.2 0.6 copy-start.29
  987.2 2.7 copy-start.5
  987.2 2.7 copy-start.11
  987.2 2.7 copy-start.16
  987.2 2.7 copy-start.21
  987.2 2.7 copy-start.23
  987.2 2.7 copy-start.27
  987.2 2.7 copy-start.30
  (1 other events, 0.5 us)
Sparse Core Ops, SparseCore 0:
  30.3 158.5 all-reduce.4
  310.6 147.3 all-reduce.6
  655.6 146.9 all-reduce.8
